TPU v7x, 32 devices: a whole 2x2x4 slice. The times are simulated.
32 devices in a mesh: groups: 2 (over x), tile: 16 (over z, y, core).
Axes of the slice: x: 2, y: 2, z: 4, core: 2. Of those that a mesh axis runs over, the one named last changes fastest.
Arguments:
- object_tiles: float32 [32, 2, 768, 768], P(('groups', 'tile')), parts along dimension 0, may hold values from -6 to 6
- probe: float32 [2, 256, 256], replicated, may hold values from -6 to 6
- intensity: bfloat16 [1024, 256, 256], P(('groups', 'tile')), parts along dimension 0, may hold values from 0 to 8
- counts: int32 [32], P(('groups', 'tile')), parts along dimension 0, may hold values from 1 to 32, 256 in all
- offsets: int32 [1024, 2], P(('groups', 'tile')), parts along dimension 0, may hold values from 0 to 767, as said below
Outputs:
- object_new: float32 [32, 2, 768, 768], P(('groups', 'tile')), parts along dimension 0
- probe_step: float32 [4, 256, 256], P('groups'), parts along dimension 0
There are 2 independent parts, one for each index of `groups`. A program takes and returns all parts, laid end to end along the dimension named above; an argument that names none is the same for every part. Nothing has to cross between parts.
Inputs may be any that keep to these rules, and one draw needn't show every extreme that they name: `counts`: live patterns of a tile; some tile has exactly 32. `offsets`: pixel offset of a window within its tile; 767 occurs in every draw.
All inputs are finite; a program needn't handle non-finite values. No bound on the sum of `counts` on one device may be relied on, other than what follows from the above.
Results may differ from a plain program's by a relative error of at most 0.0049.
Values sent between devices are 32-bit elements; how exact they have to be, the bound alone decides.
A program may use at most 192 MiB of HBM per device.

v0:
```python
import functools
import math

import jax
import jax.numpy as jnp
from jax import lax
from jax.experimental import pallas as pl
from jax.experimental.pallas import tpu as pltpu
from jax.sharding import PartitionSpec as P

floor_amp = 0.5
object_damp = 0.5
probe_damp = 1.0
LANE = 128
CHUNK = 32


def passed_along(value, axis, down, across):
    count = lax.axis_size(axis)
    cols = count // 2
    pairs = []
    for source in range(count):
        row, col = source // cols + down, source % cols + across
        if 0 <= row < 2 and 0 <= col < cols:
            pairs.append((source, row * cols + col))
    return lax.ppermute(value, axis, pairs)


def dft_tables(window):
    steps = jnp.arange(window, dtype=jnp.int32)
    phase = steps[:, None] * steps[None, :] % window
    angle = phase.astype(jnp.float32) * (2.0 * math.pi / window)
    scale = 1.0 / math.sqrt(window)
    return (
        (jnp.cos(angle) * scale).astype(jnp.bfloat16),
        (-jnp.sin(angle) * scale).astype(jnp.bfloat16),
    )


def scatter_block(acc, ch, k0, row, size, q, shift, keep):
    turned = [pltpu.roll(v, shift, 1) for v in q]
    count = len(q)
    for b in range(count + 1):
        if b == 0:
            value = jnp.where(keep, turned[0], 0.0)
        elif b == count:
            value = jnp.where(keep, 0.0, turned[count - 1])
        else:
            value = jnp.where(keep, turned[b], turned[b - 1])
        at = (ch, k0 + b, pl.ds(row, size), slice(None))
        acc[at] = acc[at] + value


def pattern_kernel(plan, window, row_base, low, high, n_part, *refs):
    offs, cnt, probe, tab_a, tab_b, intensity, earlier = refs[:7]
    parts = refs[7 : 7 + n_part]
    out, sums, mark = refs[7 + n_part : 10 + n_part]
    ext, acc, win, xb, hb, big, sem_in, sem_out, sem_int, ibuf = refs[10 + n_part :]
    mark[0, 0] = jnp.float32(1.0)
    blocks = window // LANE
    copies = []
    for i, (which, rows, cols, to_row, to_col) in enumerate(plan):
        for k in range((cols[1] - cols[0]) // LANE):
            copies.append(
                pltpu.make_async_copy(
                    parts[which].at[:, pl.ds(rows[0], rows[1] - rows[0]), pl.ds(cols[0] + k * LANE, LANE)],
                    ext.at[:, to_col // LANE + k, pl.ds(to_row, rows[1] - rows[0]), :],
                    sem_in.at[len(copies)],
                )
            )
    for copy in copies:
        copy.start()
    get_int = pltpu.make_async_copy(intensity, ibuf, sem_int)
    get_int.start()
    acc[...] = jnp.zeros(acc.shape, jnp.float32)
    sums[...] = earlier[...]
    for copy in copies:
        copy.wait()
    get_int.wait()
    lane = lax.broadcasted_iota(jnp.int32, (CHUNK, LANE), 1)

    def step(slot, carry):
        row = offs[slot, 0]
        col = offs[slot, 1]

        @pl.when((row >= low) & (row < high))
        def _():
            base = row - row_base
            k0 = col // LANE
            shift = col % LANE
            back = lax.rem(LANE - shift, LANE)
            take = lane < LANE - shift
            keep = lane >= shift

            for i in range(0, window, CHUNK):
                got = []
                for ch in range(2):
                    turned = [
                        pltpu.roll(ext[ch, k0 + b, pl.ds(base + i, CHUNK), :], back, 1)
                        for b in range(blocks + 1)
                    ]
                    got.append(
                        [jnp.where(take, turned[b], turned[b + 1]) for b in range(blocks)]
                    )
                for b in range(blocks):
                    at = (slice(i, i + CHUNK), slice(b * LANE, (b + 1) * LANE))
                    wr, wi = got[0][b], got[1][b]
                    pr, pi = probe[(0,) + at], probe[(1,) + at]
                    win[(0,) + at] = wr
                    win[(1,) + at] = wi
                    sums[(2,) + at] += wr * wr + wi * wi
                    xb[at] = (pr * wr - pi * wi).astype(jnp.bfloat16)
                    xb[slice(window + i, window + i + CHUNK), at[1]] = (pr * wi + pi * wr).astype(
                        jnp.bfloat16
                    )
            half = jnp.dot(tab_a[...], xb[...], preferred_element_type=jnp.float32)
            hb[:, :window] = half[:window].astype(jnp.bfloat16)
            hb[:, window:] = half[window:].astype(jnp.bfloat16)
            big[...] = jnp.dot(hb[...], tab_b[...], preferred_element_type=jnp.float32)
            for i in range(0, window, CHUNK):
                re = big[i : i + CHUNK, :window]
                im = big[i : i + CHUNK, window:]
                power = jnp.maximum(re * re + im * im, floor_amp * floor_amp)
                seen = ibuf[slot, i : i + CHUNK, :].astype(jnp.float32)
                factor = jnp.sqrt(seen) * lax.rsqrt(power) - 1.0
                xb[i : i + CHUNK, :] = (re * factor).astype(jnp.bfloat16)
                xb[window + i : window + i + CHUNK, :] = (im * factor).astype(jnp.bfloat16)
            half = jnp.dot(tab_b[...], xb[...], preferred_element_type=jnp.float32)
            hb[:, :window] = half[:window].astype(jnp.bfloat16)
            hb[:, window:] = half[window:].astype(jnp.bfloat16)
            big[...] = jnp.dot(hb[...], tab_a[...], preferred_element_type=jnp.float32)
            for i in range(0, window, CHUNK):
                g_re, g_im = [], []
                for b in range(blocks):
                    at = (slice(i, i + CHUNK), slice(b * LANE, (b + 1) * LANE))
                    cr = big[at]
                    ci = big[slice(i, i + CHUNK), window + b * LANE : window + (b + 1) * LANE]
                    pr, pi = probe[(0,) + at], probe[(1,) + at]
                    wr, wi = win[(0,) + at], win[(1,) + at]
                    g_re.append(pr * cr + pi * ci)
                    g_im.append(pr * ci - pi * cr)
                    sums[(0,) + at] += wr * cr + wi * ci
                    sums[(1,) + at] += wr * ci - wi * cr
                scatter_block(acc, 0, k0, base + i, CHUNK, g_re, shift, keep)
                scatter_block(acc, 1, k0, base + i, CHUNK, g_im, shift, keep)

        return carry

    lax.fori_loop(0, cnt[0], step, 0)
    ends = []
    for ch in range(2):
        for k in range(acc.shape[1]):
            ends.append(
                pltpu.make_async_copy(
                    acc.at[ch, k], out.at[ch, :, pl.ds(k * LANE, LANE)], sem_out.at[ch, k]
                )
            )
    for copy in ends:
        copy.start()
    for copy in ends:
        copy.wait()


def run_patterns(plan, parts, offsets, counts, probe, tab_a, tab_b, intensity, earlier, row_base, rows, low, high, width):
    window = probe.shape[1]
    slots = intensity.shape[0]
    n_copy = sum((c[1] - c[0]) // LANE for _, _, c, _, _ in plan)
    smem = pl.BlockSpec(memory_space=pltpu.SMEM)
    vmem = pl.BlockSpec(memory_space=pltpu.VMEM)
    anys = pl.BlockSpec(memory_space=pl.ANY)
    n_block = width // LANE
    return pl.pallas_call(
        functools.partial(pattern_kernel, plan, window, row_base, low, high, len(parts)),
        out_shape=(
            jax.ShapeDtypeStruct((2, rows, width), jnp.float32),
            jax.ShapeDtypeStruct((3, window, window), jnp.float32),
            jax.ShapeDtypeStruct((1, 1), jnp.float32),
        ),
        in_specs=[smem, smem, vmem, vmem, vmem, anys, vmem] + [anys] * len(parts),
        out_specs=(anys, vmem, smem),
        scratch_shapes=[
            pltpu.VMEM((2, n_block, rows, LANE), jnp.float32),
            pltpu.VMEM((2, n_block, rows, LANE), jnp.float32),
            pltpu.VMEM((2, window, window), jnp.float32),
            pltpu.VMEM((2 * window, window), jnp.bfloat16),
            pltpu.VMEM((window, 2 * window), jnp.bfloat16),
            pltpu.VMEM((window, 2 * window), jnp.float32),
            pltpu.SemaphoreType.DMA((n_copy,)),
            pltpu.SemaphoreType.DMA((2, n_block)),
            pltpu.SemaphoreType.DMA,
            pltpu.VMEM((slots, window, window), jnp.bfloat16),
        ],
        compiler_params=pltpu.CompilerParams(vmem_limit_bytes=44 << 20),
        cost_estimate=pl.CostEstimate(
            flops=slots * 16 * window**3, bytes_accessed=30 << 20, transcendentals=0
        ),
    )(offsets, counts, probe, tab_a, tab_b, intensity, earlier, *parts)


def weight_kernel(window, tile, offs, cnt, probe, out, acc, power, sem):
    blocks = window // LANE
    acc[...] = jnp.zeros(acc.shape, jnp.float32)
    power[...] = probe[0] * probe[0] + probe[1] * probe[1]
    lane = lax.broadcasted_iota(jnp.int32, (CHUNK, LANE), 1)
    slots = offs.shape[1]
    for source in range(4):
        down, across = source // 2, source % 2

        def step(slot, carry):
            row = offs[source, slot, 0] - down * tile + window
            col = offs[source, slot, 1] - across * tile + window

            @pl.when((row > 0) & (col > 0))
            def _():
                k0 = col // LANE
                shift = col % LANE
                keep = lane >= shift
                for i in range(0, window, CHUNK):
                    q = [power[i : i + CHUNK, b * LANE : (b + 1) * LANE] for b in range(blocks)]
                    scatter_block(acc, 0, k0, row + i, CHUNK, q, shift, keep)

            return carry

        lax.fori_loop(0, cnt[source, 0], step, 0)
    ends = [
        pltpu.make_async_copy(
            acc.at[0, blocks + k, pl.ds(window, tile), :], out.at[:, pl.ds(k * LANE, LANE)], sem.at[k]
        )
        for k in range(tile // LANE)
    ]
    for copy in ends:
        copy.start()
    for copy in ends:
        copy.wait()


def weights(offs, cnt, probe, tile):
    window = probe.shape[1]
    side = tile + 2 * window
    smem = pl.BlockSpec(memory_space=pltpu.SMEM)
    vmem = pl.BlockSpec(memory_space=pltpu.VMEM)
    return pl.pallas_call(
        functools.partial(weight_kernel, window, tile),
        out_shape=jax.ShapeDtypeStruct((tile, tile), jnp.float32),
        in_specs=[smem, smem, vmem],
        out_specs=pl.BlockSpec(memory_space=pl.ANY),
        scratch_shapes=[
            pltpu.VMEM((1, side // LANE, side, LANE), jnp.float32),
            pltpu.VMEM((window, window), jnp.float32),
            pltpu.SemaphoreType.DMA((tile // LANE,)),
        ],
        compiler_params=pltpu.CompilerParams(vmem_limit_bytes=16 << 20),
        cost_estimate=pl.CostEstimate(flops=8 << 30, bytes_accessed=20 << 20, transcendentals=0),
    )(offs, cnt, probe)


def join_kernel(obj, acc_1, acc_2, side_1, side_2, weight, out):
    tile = obj.shape[2]
    window = side_1.shape[2]
    i = pl.program_id(0)
    last = (i == pl.num_programs(0) - 1).astype(jnp.float32)
    for r in range(0, window, CHUNK):
        rows = slice(r, r + CHUNK)
        scale = 1.0 / (weight[rows, :] + object_damp)
        for ch in range(2):
            left = acc_1[ch, rows, :window] + side_1[ch, rows, :]
            left += last * (acc_2[ch, rows, :window] + side_2[ch, rows, :])
            rest = acc_1[ch, rows, window:tile] + last * acc_2[ch, rows, window:tile]
            total = jnp.concatenate([left, rest], axis=1)
            out[ch, rows, :] = jnp.where(i == 0, total, obj[ch, rows, :] + total * scale)


def join(obj, acc_1, acc_2, side_1, side_2, weight):
    tile = obj.shape[1]
    window = side_1.shape[2]
    side = tile + window
    moving = lambda i: (0, i, 0)
    fixed = lambda i: (0, 0, 0)
    return pl.pallas_call(
        join_kernel,
        grid=(tile // window,),
        out_shape=jax.ShapeDtypeStruct(obj.shape, jnp.float32),
        in_specs=[
            pl.BlockSpec((2, window, tile), moving),
            pl.BlockSpec((2, window, side), moving),
            pl.BlockSpec((2, window, side), fixed),
            pl.BlockSpec((2, window, window), moving),
            pl.BlockSpec((2, window, window), fixed),
            pl.BlockSpec((window, tile), lambda i: (i, 0)),
        ],
        out_specs=pl.BlockSpec((2, window, tile), moving),
        compiler_params=pltpu.CompilerParams(vmem_limit_bytes=40 << 20),
        cost_estimate=pl.CostEstimate(flops=8 << 20, bytes_accessed=22 << 20, transcendentals=0),
    )(obj, acc_1, acc_2, side_1, side_2, weight)


def finish_kernel(partial, obj, lower_a, lower_b, weight, totals, out, probe_step):
    window = lower_a.shape[1]
    for r in range(0, window, CHUNK):
        rows = slice(r, r + CHUNK)
        scale = 1.0 / (weight[rows, :] + object_damp)
        for ch in range(2):
            lower = jnp.concatenate([lower_a[ch, rows, :], lower_b[ch, rows, :]], axis=1)
            out[ch, rows, :] = obj[ch, rows, :] + (partial[ch, rows, :] + lower) * scale
        damped = 1.0 / (totals[2, rows, :] + probe_damp)
        for ch in range(2):
            probe_step[ch, rows, :] = totals[ch, rows, :] * damped


def finish(partial, obj, lower_a, lower_b, weight, totals):
    tile = obj.shape[1]
    window = lower_a.shape[1]
    fixed = lambda i: (0, 0, 0)
    strip = pl.BlockSpec((2, window, tile), fixed)
    return pl.pallas_call(
        finish_kernel,
        grid=(1,),
        out_shape=(
            jax.ShapeDtypeStruct(obj.shape, jnp.float32),
            jax.ShapeDtypeStruct((2, window, window), jnp.float32),
        ),
        in_specs=[
            strip,
            strip,
            pl.BlockSpec(lower_a.shape, fixed),
            pl.BlockSpec(lower_b.shape, fixed),
            pl.BlockSpec((window, tile), lambda i: (0, 0)),
            pl.BlockSpec(totals.shape, fixed),
        ],
        out_specs=(strip, pl.BlockSpec((2, window, window), fixed)),
        input_output_aliases={0: 0},
        compiler_params=pltpu.CompilerParams(vmem_limit_bytes=32 << 20),
        cost_estimate=pl.CostEstimate(flops=4 << 20, bytes_accessed=10 << 20, transcendentals=0),
    )(partial, obj, lower_a, lower_b, weight, totals)


def on_device(object_tiles, probe, intensity, counts, offsets):
    window = probe.shape[1]
    tile = object_tiles.shape[2]
    object_tile = object_tiles[0]
    strip = passed_along(object_tile[:, :, :window], "tile", 0, -1)
    rim_a = passed_along(object_tile[:, :window, :window], "tile", -1, 0)
    rim_b = passed_along(object_tile[:, :window, window:], "tile", -1, 0)
    where = jnp.concatenate([offsets.reshape(-1), counts])
    where_left = passed_along(where, "tile", 0, 1)
    pair = jnp.stack([where, where_left])
    pair_up = passed_along(pair, "tile", 1, 0)
    four = jnp.concatenate([pair, pair_up], axis=0)
    offs4 = four[:, :-1].reshape(4, -1, 2)
    cnt4 = four[:, -1:]

    table_re, table_im = dft_tables(window)
    tab_a = jnp.block([[table_re, -table_im], [table_im, table_re]])
    tab_b = jnp.block([[table_re, table_im], [-table_im, table_re]])
    cut = tile - window
    side = tile + window
    nothing = jnp.zeros((3, window, window), jnp.float32)
    acc_1, sums_1, mark = run_patterns(
        ((0, (0, tile), (0, tile), 0, 0), (1, (0, tile), (0, window), 0, tile)),
        (object_tile, strip),
        offsets, counts, probe, tab_a, tab_b, intensity, nothing, 0, tile, 0, cut + 1, side,
    )
    corner = passed_along(rim_a * mark[0, 0], "tile", 0, -1)
    side_1 = passed_along(acc_1[:, :, tile:], "tile", 0, 1)
    weight = weights(offs4, cnt4, probe, tile)
    acc_2, sums, _ = run_patterns(
        (
            (0, (cut, tile), (0, tile), 0, 0),
            (1, (cut, tile), (0, window), 0, tile),
            (2, (0, window), (0, window), window, 0),
            (3, (0, window), (0, tile - window), window, window),
            (4, (0, window), (0, window), window, tile),
        ),
        (object_tile, strip, rim_a, rim_b, corner),
        offsets, counts, probe, tab_a, tab_b, intensity, sums_1, cut, 2 * window, cut + 1, tile, side,
    )
    side_2 = passed_along(acc_2[:, :, tile:], "tile", 0, 1)
    lower_b = passed_along(acc_2[:, window:, window:tile], "tile", 1, 0)
    totals = lax.psum(sums, "tile")
    lower_a = passed_along(acc_2[:, window:, :window] + side_2[:, window:], "tile", 1, 0)
    partial = join(object_tile, acc_1, acc_2, side_1, side_2, weight)
    object_new, probe_step = finish(partial, object_tile, lower_a, lower_b, weight, totals)
    return (object_new[None], probe_step)


def solution(mesh):
    in_specs = (
        P(("groups", "tile"), None, None, None),
        P(),
        P(("groups", "tile"), None, None),
        P(("groups", "tile")),
        P(("groups", "tile"), None),
    )
    out_specs = (P(("groups", "tile"), None, None, None), P("groups", None, None))
    return jax.shard_map(
        on_device, mesh=mesh, in_specs=in_specs, out_specs=out_specs, check_vma=False
    )
```

profile of v0, /device:TPU:0, one launch (start us, length us, event | category | flops | bytes accessed | tf_op | source)
XLA Modules:
  0.0 311.0 jit_solution(313343402664208226)
XLA Ops:
  7.2 0.0 copy-start.6
  7.2 0.0 all-reduce.2.cloned.1.call-start
  7.2 2.7 slice.40
  9.9 1.3 collective-permute-start
  11.2 1.9 slice.41
  13.0 1.3 collective-permute-start.1
  14.3 2.3 slice.42
  16.6 1.3 collective-permute-start.2
  17.9 0.0 copy-done.6
  17.9 0.1 copy.11.refs_0_
  18.6 1.0 fusion.8
  19.6 1.1 multiply_convert_fusion
  20.7 0.1 fusion.1
  20.8 0.0 collective-permute-done.refs_8_
  20.8 0.1 broadcast_in_dim.8.refs_6_
  20.9 0.0 copy-start.3
  20.9 2.2 copy-done.3
  23.1 0.0 copy-start.4
  23.1 1.0 copy-done.4
  24.1 50.0 %shard_map.68 = (f32[2,768,1024]{2,1,0:T(8,128)}, f32[3,256,256]{2,1,0:T(8,128)S(1)}, f32[1,1]{1,0:T(1,128)}) custom-call(s32[32,2]{1,0:T(8,128)S(1)} %copy.11.refs_0_, s32[1]{0:T(128)S(6)} %copy.18.refs_1_, f32[2,256,256]{2,1,0:T(8,128)S(1)} %copy-done.4, bf16[512,512]{1,0:T(8,128)(2,1)S(1)} %get-tuple-element.17.refs_3_, ...), custom_call_target="tpu_custom_call" | custom-call | flops 8589934592 | bytes 31457280 | tf_op jit(solution)/shard_map/pallas_call | solution.py:172
  74.2 0.0 collective-permute-done.1.refs_9_
  74.2 0.7 broadcast_multiply_fusion
  74.9 1.3 collective-permute-start.3
  76.2 11.1 %collective-permute-done.2.refs_10_ = f32[2,256,512]{2,1,0:T(8,128)S(1)} collective-permute-done((f32[2,256,512]{2,1,0:T(8,128)}, f32[2,256,512]{2,1,0:T(8,128)S(1)}, u32[]{:S(2)}, u32[]{:S(2)}) %collective-permute-start.2) | collective-permute-done | bytes 1048608 | tf_op jit(solution)/shard_map/ppermute | solution.py:26
  87.3 0.0 collective-permute-done.3.refs_11_
  87.3 24.1 %shard_map.69 = (f32[2,512,1024]{2,1,0:T(8,128)}, f32[3,256,256]{2,1,0:T(8,128)}, f32[1,1]{1,0:T(1,128)}) custom-call(s32[32,2]{1,0:T(8,128)S(1)} %copy.11.refs_0_, s32[1]{0:T(128)S(6)} %copy.18.refs_1_, f32[2,256,256]{2,1,0:T(8,128)S(1)} %copy-done.4, bf16[512,512]{1,0:T(8,128)(2,1)S(1)} %get-tuple-element.17.refs_3_, ...), custom_call_target="tpu_custom_call" | custom-call | flops 8589934592 | bytes 31457280 | tf_op jit(solution)/shard_map/pallas_call | solution.py:172
  111.4 1.3 slice.34
  112.7 1.4 collective-permute-start.5
  114.0 2.8 slice.33
  116.8 2.4 collective-permute-start.4
  119.2 0.1 reshape.10
  119.3 0.1 pad_add_fusion.2
  119.4 1.3 collective-permute-start.6
  120.7 0.1 fusion.9
  120.8 0.7 collective-permute-done.6
  121.5 2.9 collective-permute-start.7
  124.5 1.3 collective-permute-done.7
  125.7 0.1 slice.36.cnt
  125.8 0.1 copy.14
  125.9 0.3 copy.15.offs
  126.3 2.3 slice.39
  128.5 6.1 %collective-permute-start.9 = (f32[2,256,512]{2,1,0:T(8,128)}, f32[2,256,512]{2,1,0:T(8,128)}, u32[]{:S(2)}, u32[]{:S(2)}) collective-permute-start(f32[2,256,512]{2,1,0:T(8,128)} %slice.39), channel_id=1, source_target_pairs={{0,8},{1,9},{2,10},{3,11},{4,12},{5,13},{6,14},{7,15},{16,24},{17,... | collective-permute-start | bytes 3145736 | tf_op jit(solution)/shard_map/ppermute | solution.py:26
  134.6 0.0 all-reduce.2.cloned.1.call-update
  134.6 0.0 collective-permute-done.5.side_2
  134.6 0.0 slice-start
  134.7 2.1 slice_add_fusion
  136.7 0.0 slice-start.1
  136.7 0.0 copy-start.1
  136.7 2.3 collective-permute-start.8
  139.1 0.0 copy-start.5
  139.1 1.0 copy-done.5
  140.1 7.0 %shard_map.70.weight = f32[768,768]{1,0:T(8,128)S(1)} custom-call(s32[4,32,2]{2,1,0:T(8,128)S(1)} %copy.15.offs, s32[4,1]{1,0:T(4,128)S(1)} %slice.36.cnt, f32[2,256,256]{2,1,0:T(8,128)S(1)} %copy-done.5), custom_call_target="tpu_custom_call" | custom-call | flops 8589934592 | bytes 20971520 | tf_op jit(solution)/shard_map/pallas_call | solution.py:242
  147.2 0.0 collective-permute-done.4.side_1
  147.2 0.0 slice-done
  147.2 0.0 slice-done.1
  147.2 0.0 copy-done.1
  147.2 6.6 %shard_map.71.partial = f32[2,768,768]{2,1,0:T(8,128)} custom-call(f32[2,768,768]{2,1,0:T(8,128)S(1)} %bitcast.15, f32[2,768,1024]{2,1,0:T(8,128)} %get-tuple-element.9.acc_1, f32[2,512,1024]{2,1,0:T(8,128)S(1)} %copy-done.1, f32[2,768,256]{2,1,0:T(8,128)} %collective-permute-done.4.side_1, f32[2,512,256]{2,1,0:T(8,128)S(1)} %collective-permute-done.5.side_2, ...), custom_call_target="tpu_custom_call" | custom-call | flops 8388608 | bytes 23068672 | tf_op jit(solution)/shard_map/pallas_call | solution.py:279
  153.8 143.5 %all-reduce.2.cloned.1.call-done.totals = f32[3,256,256]{2,1,0:T(8,128)} async-done(((f32[3,256,256]{2,1,0:T(8,128)}), f32[3,256,256]{2,1,0:T(8,128)}) %all-reduce.2.cloned.1.call-update) | async-done | bytes 786448 | tf_op jit(solution)/shard_map/psum | solution.py:379
  297.2 0.0 collective-permute-done.9.lower_b
  297.2 0.0 collective-permute-done.8.lower_a
  297.2 0.0 copy-start
  297.2 2.3 copy-done
  299.6 1.1 copy-done.2
  300.7 3.5 %shard_map.72 = (f32[2,768,768]{2,1,0:T(8,128)}, f32[2,256,256]{2,1,0:T(8,128)}) custom-call(f32[2,768,768]{2,1,0:T(8,128)} %shard_map.71.partial, f32[2,768,768]{2,1,0:T(8,128)S(1)} %bitcast.16, f32[2,256,256]{2,1,0:T(8,128)} %collective-permute-done.8.lower_a, f32[2,256,512]{2,1,0:T(8,128)} %collective-permute-done.9.lower_b, ...), custom_call_target="tpu_custom_call", output_to_operand_aliasing={{0}: (0, {})} | custom-call | flops 4194304 | bytes 10485760 | tf_op jit(solution)/shard_map/pallas_call | solution.py:315
  (4 shorter events, 0.0 us)
Async XLA Ops:
  7.2 10.7 %copy-start.6 = (s32[32,2]{0,1:T(2,128)S(1)}, s32[32,2]{0,1:T(2,128)}, u32[]{:S(2)}) copy-start(s32[32,2]{0,1:T(2,128)} %param.9) | copy-start | bytes 772
  7.2 290.1 %all-reduce.2.cloned.1.call-start = ((), (), s32[]{:S(2)}) async-start(), calls=%async_computation | async-start | bytes 1572864 | tf_op jit(solution)/shard_map/psum | solution.py:379
  9.9 11.0 %collective-permute-start = (f32[2,768,256]{2,1,0:T(8,128)}, f32[2,768,256]{2,1,0:T(8,128)S(1)}, u32[]{:S(2)}, u32[]{:S(2)}) collective-permute-start(f32[2,768,256]{2,1,0:T(8,128)} %slice.40), channel_id=1, source_target_pairs={{1,0},{2,1},{3,2},{4,3},{5,4},{6,5},{7,6},{9,8},{10,9},{11,10},{12... | collective-permute-start | bytes 4718600 | tf_op jit(solution)/shard_map/ppermute | solution.py:26
  13.0 61.2 %collective-permute-start.1 = (f32[2,256,256]{2,1,0:T(8,128)}, f32[2,256,256]{2,1,0:T(8,128)S(1)}, u32[]{:S(2)}, u32[]{:S(2)}) collective-permute-start(f32[2,256,256]{2,1,0:T(8,128)} %slice.41), channel_id=1, source_target_pairs={{8,0},{9,1},{10,2},{11,3},{12,4},{13,5},{14,6},{15,7},{24,16},{25,... | collective-permute-start | bytes 1572872 | tf_op jit(solution)/shard_map/ppermute | solution.py:26
  16.6 70.7 %collective-permute-start.2 = (f32[2,256,512]{2,1,0:T(8,128)}, f32[2,256,512]{2,1,0:T(8,128)S(1)}, u32[]{:S(2)}, u32[]{:S(2)}) collective-permute-start(f32[2,256,512]{2,1,0:T(8,128)} %slice.42), channel_id=1, source_target_pairs={{8,0},{9,1},{10,2},{11,3},{12,4},{13,5},{14,6},{15,7},{24,16},{25,... | collective-permute-start | bytes 3145736 | tf_op jit(solution)/shard_map/ppermute | solution.py:26
  20.9 2.2 copy-start.3
  23.1 1.0 copy-start.4
  74.9 12.4 %collective-permute-start.3 = (f32[2,256,256]{2,1,0:T(8,128)S(1)}, f32[2,256,256]{2,1,0:T(8,128)S(1)}, u32[]{:S(2)}, u32[]{:S(2)}) collective-permute-start(f32[2,256,256]{2,1,0:T(8,128)S(1)} %broadcast_multiply_fusion), channel_id=1, source_target_pairs={{1,0},{2,1},{3,2},{4,3},{5,4},{6,5},{7,6},{9,8},{10,9},{11,10},{12... | collective-permute-start | bytes 1572872 | tf_op jit(solution)/shard_map/ppermute | solution.py:26
  112.7 22.0 %collective-permute-start.5 = (f32[2,512,256]{2,1,0:T(8,128)S(1)}, f32[2,512,256]{2,1,0:T(8,128)S(1)}, u32[]{:S(2)}, u32[]{:S(2)}) collective-permute-start(f32[2,512,256]{2,1,0:T(8,128)S(1)} %slice.34), channel_id=1, source_target_pairs={{0,1},{1,2},{2,3},{3,4},{4,5},{5,6},{6,7},{8,9},{9,10},{10,11},{11... | collective-permute-start | bytes 3145736 | tf_op jit(solution)/shard_map/ppermute | solution.py:26
  116.8 30.4 %collective-permute-start.4 = (f32[2,768,256]{2,1,0:T(8,128)}, f32[2,768,256]{2,1,0:T(8,128)}, u32[]{:S(2)}, u32[]{:S(2)}) collective-permute-start(f32[2,768,256]{2,1,0:T(8,128)} %slice.33), channel_id=1, source_target_pairs={{0,1},{1,2},{2,3},{3,4},{4,5},{5,6},{6,7},{8,9},{9,10},{10,11},{11... | collective-permute-start | bytes 4718600 | tf_op jit(solution)/shard_map/ppermute | solution.py:26
  119.4 2.1 collective-permute-start.6
  121.5 4.2 %collective-permute-start.7 = (s32[2,65]{1,0:T(2,128)S(1)}, s32[2,65]{1,0:T(2,128)S(1)}, u32[]{:S(2)}, u32[]{:S(2)}) collective-permute-start(s32[2,65]{1,0:T(2,128)S(1)} %pad_add_fusion.1), channel_id=1, source_target_pairs={{0,8},{1,9},{2,10},{3,11},{4,12},{5,13},{6,14},{7,15},{16,24},{17,... | collective-permute-start | bytes 1568 | tf_op jit(solution)/shard_map/ppermute | solution.py:26
  128.5 168.7 %collective-permute-start.9 = (f32[2,256,512]{2,1,0:T(8,128)}, f32[2,256,512]{2,1,0:T(8,128)}, u32[]{:S(2)}, u32[]{:S(2)}) collective-permute-start(f32[2,256,512]{2,1,0:T(8,128)} %slice.39), channel_id=1, source_target_pairs={{0,8},{1,9},{2,10},{3,11},{4,12},{5,13},{6,14},{7,15},{16,24},{17,... | collective-permute-start | bytes 3145736 | tf_op jit(solution)/shard_map/ppermute | solution.py:26
  134.6 12.5 %slice-start = ((s8[4718592]{0:T(1024)(128)(4,1)}), s8[4194304]{0:T(1024)(128)(4,1)S(1)}, s32[]{:S(2)}) async-start(s8[4718592]{0:T(1024)(128)(4,1)} %bitcast.13), calls=%async_computation.1 | async-start | bytes 8388608
  136.7 10.4 %slice-start.1 = ((s8[4718592]{0:T(1024)(128)(4,1)}), s8[524288]{0:T(1024)(128)(4,1)S(1)}, s32[]{:S(2)}) async-start(s8[4718592]{0:T(1024)(128)(4,1)} %bitcast.13), calls=%async_computation.2 | async-start | bytes 1048576
  136.7 10.5 %copy-start.1 = (f32[2,512,1024]{2,1,0:T(8,128)S(1)}, f32[2,512,1024]{2,1,0:T(8,128)}, u32[]{:S(2)}) copy-start(f32[2,512,1024]{2,1,0:T(8,128)} %get-tuple-element.12.acc_2) | copy-start | bytes 12582916
  136.7 160.5 %collective-permute-start.8 = (f32[2,256,256]{2,1,0:T(8,128)}, f32[2,256,256]{2,1,0:T(8,128)}, u32[]{:S(2)}, u32[]{:S(2)}) collective-permute-start(f32[2,256,256]{2,1,0:T(8,128)} %slice_add_fusion), channel_id=1, source_target_pairs={{0,8},{1,9},{2,10},{3,11},{4,12},{5,13},{6,14},{7,15},{16,24},{17,... | collective-permute-start | bytes 1572872 | tf_op jit(solution)/shard_map/ppermute | solution.py:26
  139.1 1.0 copy-start.5
  297.2 2.3 copy-start
  299.6 1.1 copy-start.2
Sparse Core Ops, SparseCore 0:
  134.8 162.4 all-reduce.1
where the time goes:
time: 314 us; the launch traced here: 311 us
  waiting for transfers between devices  157 us (50%)
  Pallas kernels  91.2 us (29%)
  local copies, waits for them, and re-layouts  21.7 us (7%)
  starting transfers between devices  21.6 us (7%)
  between operations  14.9 us (5%)
  other arithmetic  5.1 us (2%)
    psum x1, waiting for transfers between devices, on_device(): totals = lax.psum(sums, 'tile')  143 us
    pallas_call x2, Pallas kernels, run_patterns(): pl.pallas_call(functools.partial(pattern_kernel, plan, window, row_base,...  74.1 us
    ppermute x10, starting transfers between devices, passed_along(): return lax.ppermute(value, axis, pairs)  21.6 us
    ppermute x10, waiting for transfers between devices, passed_along(): return lax.ppermute(value, axis, pairs)  13.1 us
    unnamed x19, local copies, waits for them, and re-layouts  7.84 us
    pallas_call x1, Pallas kernels, weights(): pl.pallas_call(functools.partial(weight_kernel, window, tile), out_shape=...  7.03 us
    pallas_call x1, Pallas kernels, join(): pl.pallas_call(join_kernel, grid=(tile // window,), out_shape=jax.ShapeDt...  6.58 us
  transfers between devices with their start and end apart: 11, of which 4 were waited for; matrix products, arithmetic and copies ran while one was open for 5% of the time, Pallas kernels for 20%

commit v1 on v0

--- a/solution.py
+++ b/solution.py
@@ -52,10 +52,10 @@
 
 
 def pattern_kernel(plan, window, row_base, low, high, n_part, *refs):
-    offs, cnt, probe, tab_a, tab_b, intensity, earlier = refs[:7]
-    parts = refs[7 : 7 + n_part]
-    out, sums, mark = refs[7 + n_part : 10 + n_part]
-    ext, acc, win, xb, hb, big, sem_in, sem_out, sem_int, ibuf = refs[10 + n_part :]
+    offs, cnt, probe, tab_a, tab_b, intensity, earlier, _ = refs[:8]
+    parts = refs[8 : 8 + n_part]
+    out, sums, mark = refs[8 + n_part : 11 + n_part]
+    ext, acc, win, xb, hb, big, sem_in, sem_out, sem_int, ibuf = refs[11 + n_part :]
     mark[0, 0] = jnp.float32(1.0)
     blocks = window // LANE
     copies = []
@@ -161,7 +161,7 @@
         copy.wait()
 
 
-def run_patterns(plan, parts, offsets, counts, probe, tab_a, tab_b, intensity, earlier, row_base, rows, low, high, width):
+def run_patterns(plan, parts, offsets, counts, probe, tab_a, tab_b, intensity, earlier, after, row_base, rows, low, high, width):
     window = probe.shape[1]
     slots = intensity.shape[0]
     n_copy = sum((c[1] - c[0]) // LANE for _, _, c, _, _ in plan)
@@ -176,7 +176,7 @@
             jax.ShapeDtypeStruct((3, window, window), jnp.float32),
             jax.ShapeDtypeStruct((1, 1), jnp.float32),
         ),
-        in_specs=[smem, smem, vmem, vmem, vmem, anys, vmem] + [anys] * len(parts),
+        in_specs=[smem, smem, vmem, vmem, vmem, anys, vmem, smem] + [anys] * len(parts),
         out_specs=(anys, vmem, smem),
         scratch_shapes=[
             pltpu.VMEM((2, n_block, rows, LANE), jnp.float32),
@@ -194,7 +194,7 @@
         cost_estimate=pl.CostEstimate(
             flops=slots * 16 * window**3, bytes_accessed=30 << 20, transcendentals=0
         ),
-    )(offsets, counts, probe, tab_a, tab_b, intensity, earlier, *parts)
+    )(offsets, counts, probe, tab_a, tab_b, intensity, earlier, after, *parts)
 
 
 def weight_kernel(window, tile, offs, cnt, probe, out, acc, power, sem):
@@ -338,16 +338,20 @@
     window = probe.shape[1]
     tile = object_tiles.shape[2]
     object_tile = object_tiles[0]
+    where = jnp.concatenate([offsets.reshape(-1), counts])
+    four = jnp.stack(
+        [
+            where,
+            passed_along(where, "tile", 0, 1),
+            passed_along(where, "tile", 1, 0),
+            passed_along(where, "tile", 1, 1),
+        ]
+    )
+    offs4 = four[:, :-1].reshape(4, -1, 2)
+    cnt4 = four[:, -1:]
     strip = passed_along(object_tile[:, :, :window], "tile", 0, -1)
     rim_a = passed_along(object_tile[:, :window, :window], "tile", -1, 0)
     rim_b = passed_along(object_tile[:, :window, window:], "tile", -1, 0)
-    where = jnp.concatenate([offsets.reshape(-1), counts])
-    where_left = passed_along(where, "tile", 0, 1)
-    pair = jnp.stack([where, where_left])
-    pair_up = passed_along(pair, "tile", 1, 0)
-    four = jnp.concatenate([pair, pair_up], axis=0)
-    offs4 = four[:, :-1].reshape(4, -1, 2)
-    cnt4 = four[:, -1:]
 
     table_re, table_im = dft_tables(window)
     tab_a = jnp.block([[table_re, -table_im], [table_im, table_re]])
@@ -358,7 +362,7 @@
     acc_1, sums_1, mark = run_patterns(
         ((0, (0, tile), (0, tile), 0, 0), (1, (0, tile), (0, window), 0, tile)),
         (object_tile, strip),
-        offsets, counts, probe, tab_a, tab_b, intensity, nothing, 0, tile, 0, cut + 1, side,
+        offsets, counts, probe, tab_a, tab_b, intensity, nothing, cnt4, 0, tile, 0, cut + 1, side,
     )
     corner = passed_along(rim_a * mark[0, 0], "tile", 0, -1)
     side_1 = passed_along(acc_1[:, :, tile:], "tile", 0, 1)
@@ -372,12 +376,13 @@
             (4, (0, window), (0, window), window, tile),
         ),
         (object_tile, strip, rim_a, rim_b, corner),
-        offsets, counts, probe, tab_a, tab_b, intensity, sums_1, cut, 2 * window, cut + 1, tile, side,
-    )
-    side_2 = passed_along(acc_2[:, :, tile:], "tile", 0, 1)
+        offsets, counts, probe, tab_a, tab_b, intensity, sums_1, cnt4, cut, 2 * window, cut + 1, tile, side,
+    )
+    below = passed_along(acc_2[:, window:, tile:], "tile", 0, 1)
     lower_b = passed_along(acc_2[:, window:, window:tile], "tile", 1, 0)
     totals = lax.psum(sums, "tile")
-    lower_a = passed_along(acc_2[:, window:, :window] + side_2[:, window:], "tile", 1, 0)
+    lower_a = passed_along(acc_2[:, window:, :window] + below, "tile", 1, 0)
+    side_2 = passed_along(acc_2[:, :window, tile:], "tile", 0, 1)
     partial = join(object_tile, acc_1, acc_2, side_1, side_2, weight)
     object_new, probe_step = finish(partial, object_tile, lower_a, lower_b, weight, totals)
     return (object_new[None], probe_step)

time: 314 us -> 289 us (0.920)
  Pallas kernels: 91.2 us -> 56.4 us
  starting transfers between devices: 21.6 us -> 46.1 us
  waiting for transfers between devices: 157 us -> 148 us
  local copies, waits for them, and re-layouts: 21.7 us -> 17.7 us
    psum x1, waiting for transfers between devices: 143 us -> 108 us  [on_device(): totals = lax.psum(sums, 'tile')]
    pallas_call x2, Pallas kernels: 74.1 us -> 42.1 us  [run_patterns(): pl.pallas_call(functools.partial(pattern_kernel, plan, window, row_base,...]
    ppermute x10 -> x12, waiting for transfers between devices: 13.1 us -> 39.1 us  [passed_along(): return lax.ppermute(value, axis, pairs)]
    ppermute x10 -> x12, starting transfers between devices: 21.6 us -> 46 us  [passed_along(): return lax.ppermute(value, axis, pairs)]
    unnamed x19 -> x17, local copies, waits for them, and re-layouts: 7.84 us -> 5.74 us
  transfers between devices with their start and end apart: 11 -> 13, of which waited for: 4 -> 3; matrix products, arithmetic and copies ran while one was open for 5% -> 5% of each run, Pallas kernels for 20% -> 13%
where the time goes in v1:
time: 289 us; the launch traced here: 288 us
  waiting for transfers between devices  148 us (51%)
  Pallas kernels  56.4 us (20%)
  starting transfers between devices  46.1 us (16%)
  local copies, waits for them, and re-layouts  17.7 us (6%)
  between operations  15.1 us (5%)
  other arithmetic  5.13 us (2%)
    psum x1, waiting for transfers between devices, on_device(): totals = lax.psum(sums, 'tile')  108 us
    ppermute x12, starting transfers between devices, passed_along(): return lax.ppermute(value, axis, pairs)  46 us
    pallas_call x2, Pallas kernels, run_patterns(): pl.pallas_call(functools.partial(pattern_kernel, plan, window, row_base,...  42.1 us
    ppermute x12, waiting for transfers between devices, passed_along(): return lax.ppermute(value, axis, pairs)  39.1 us
    pallas_call x1, Pallas kernels, join(): pl.pallas_call(join_kernel, grid=(tile // window,), out_shape=jax.ShapeDt...  6.59 us
  transfers between devices with their start and end apart: 13, of which 3 were waited for; matrix products, arithmetic and copies ran while one was open for 5% of the time, Pallas kernels for 13%

profile of v1, /device:TPU:0, one launch (start us, length us, event | category | flops | bytes accessed | tf_op | source)
XLA Modules:
  0.0 287.9 jit_solution(251556986067126638)
XLA Ops:
  7.2 0.0 all-reduce.2.cloned.1.call-start
  7.2 0.0 copy-start.4
  7.2 2.7 slice.40
  9.9 1.3 collective-permute-start.3
  11.2 0.8 copy.12.refs_0_
  12.0 0.1 reshape.10
  12.1 0.0 copy-start.3
  12.9 0.1 pad_add_fusion.1
  13.0 3.1 %collective-permute-start = (s32[65]{0:T(128)S(1)}, s32[65]{0:T(128)S(1)}, u32[]{:S(2)}, u32[]{:S(2)}) collective-permute-start(s32[65]{0:T(128)S(1)} %pad_add_fusion.1), channel_id=1, source_target_pairs={{0,1},{1,2},{2,3},{3,4},{4,5},{5,6},{6,7},{8,9},{9,10},{10,11},{11... | collective-permute-start | bytes 788 | tf_op jit(solution)/shard_map/ppermute | solution.py:26
  16.1 5.9 %collective-permute-start.1 = (s32[65]{0:T(128)S(1)}, s32[65]{0:T(128)S(1)}, u32[]{:S(2)}, u32[]{:S(2)}) collective-permute-start(s32[65]{0:T(128)S(1)} %pad_add_fusion.1), channel_id=1, source_target_pairs={{0,8},{1,9},{2,10},{3,11},{4,12},{5,13},{6,14},{7,15},{16,24},{17,... | collective-permute-start | bytes 788 | tf_op jit(solution)/shard_map/ppermute | solution.py:26
  22.1 2.0 collective-permute-start.2
  24.1 1.1 slice.41
  25.2 1.3 collective-permute-start.4
  26.5 1.0 fusion.8
  27.5 1.1 multiply_convert_fusion
  28.6 0.1 fusion.1
  28.7 0.1 fusion.9
  28.8 1.3 slice.42
  30.1 0.0 collective-permute-done
  30.1 1.3 collective-permute-start.5
  31.4 0.0 collective-permute-done.1
  31.4 0.0 collective-permute-done.2
  31.4 0.1 slice.30.refs_7_.cnt
  31.5 0.0 collective-permute-done.3.refs_9_
  31.5 0.1 broadcast_in_dim.8.refs_6_
  31.6 0.0 copy-done.4
  31.6 0.0 copy-done.3
  31.6 25.8 %shard_map.68 = (f32[2,768,1024]{2,1,0:T(8,128)}, f32[3,256,256]{2,1,0:T(8,128)S(1)}, f32[1,1]{1,0:T(1,128)}) custom-call(s32[32,2]{1,0:T(8,128)S(1)} %copy.12.refs_0_, s32[1]{0:T(128)S(6)} %copy.18.refs_1_, f32[2,256,256]{2,1,0:T(8,128)S(1)} %copy-done.4, bf16[512,512]{1,0:T(8,128)(2,1)S(1)} %get-tuple-element.19.refs_3_, ...), custom_call_target="tpu_custom_call" | custom-call | flops 8589934592 | bytes 31457280 | tf_op jit(solution)/shard_map/pallas_call | solution.py:172
  57.4 19.1 %collective-permute-done.4.refs_10_ = f32[2,256,256]{2,1,0:T(8,128)S(1)} collective-permute-done((f32[2,256,256]{2,1,0:T(8,128)S(1)}, f32[2,256,256]{2,1,0:T(8,128)S(1)}, u32[]{:S(2)}, u32[]{:S(2)}) %collective-permute-start.4) | collective-permute-done | bytes 524320 | tf_op jit(solution)/shard_map/ppermute | solution.py:26
  76.5 0.7 broadcast_multiply_fusion
  77.2 1.3 collective-permute-start.6
  78.5 20.0 %collective-permute-done.5.refs_11_ = f32[2,256,512]{2,1,0:T(8,128)S(1)} collective-permute-done((f32[2,256,512]{2,1,0:T(8,128)S(1)}, f32[2,256,512]{2,1,0:T(8,128)S(1)}, u32[]{:S(2)}, u32[]{:S(2)}) %collective-permute-start.5) | collective-permute-done | bytes 1048608 | tf_op jit(solution)/shard_map/ppermute | solution.py:26
  98.5 0.0 collective-permute-done.6.refs_12_
  98.5 16.3 %shard_map.69 = (f32[2,512,1024]{2,1,0:T(8,128)}, f32[3,256,256]{2,1,0:T(8,128)}, f32[1,1]{1,0:T(1,128)}) custom-call(s32[32,2]{1,0:T(8,128)S(1)} %copy.12.refs_0_, s32[1]{0:T(128)S(6)} %copy.18.refs_1_, f32[2,256,256]{2,1,0:T(8,128)S(1)} %copy-done.4, bf16[512,512]{1,0:T(8,128)(2,1)S(1)} %get-tuple-element.19.refs_3_, ...), custom_call_target="tpu_custom_call" | custom-call | flops 8589934592 | bytes 31457280 | tf_op jit(solution)/shard_map/pallas_call | solution.py:172
  114.8 1.1 slice.38
  115.9 1.3 collective-permute-start.9
  117.3 2.8 slice.34
  120.0 9.4 %collective-permute-start.7 = (f32[2,768,256]{2,1,0:T(8,128)}, f32[2,768,256]{2,1,0:T(8,128)}, u32[]{:S(2)}, u32[]{:S(2)}) collective-permute-start(f32[2,768,256]{2,1,0:T(8,128)} %slice.34), channel_id=1, source_target_pairs={{0,1},{1,2},{2,3},{3,4},{4,5},{5,6},{6,7},{8,9},{9,10},{10,11},{11... | collective-permute-start | bytes 4718600 | tf_op jit(solution)/shard_map/ppermute | solution.py:26
  129.4 0.1 copy.14
  129.5 0.3 copy.15.offs
  129.8 2.3 slice.39
  132.1 7.9 %collective-permute-start.11 = (f32[2,256,512]{2,1,0:T(8,128)}, f32[2,256,512]{2,1,0:T(8,128)S(1)}, u32[]{:S(2)}, u32[]{:S(2)}) collective-permute-start(f32[2,256,512]{2,1,0:T(8,128)} %slice.39), channel_id=1, source_target_pairs={{0,8},{1,9},{2,10},{3,11},{4,12},{5,13},{6,14},{7,15},{16,24},{17,... | collective-permute-start | bytes 3145736 | tf_op jit(solution)/shard_map/ppermute | solution.py:26
  140.0 0.0 all-reduce.2.cloned.1.call-update
  140.1 0.0 collective-permute-done.9
  140.1 2.1 slice_add_fusion
  142.2 8.8 %collective-permute-start.8 = (f32[2,256,256]{2,1,0:T(8,128)S(1)}, f32[2,256,256]{2,1,0:T(8,128)S(1)}, u32[]{:S(2)}, u32[]{:S(2)}) collective-permute-start(f32[2,256,256]{2,1,0:T(8,128)S(1)} %get-tuple-element.17), channel_id=1, source_target_pairs={{0,1},{1,2},{2,3},{3,4},{4,5},{5,6},{6,7},{8,9},{9,10},{10,11},{11... | collective-permute-start | bytes 1572872 | tf_op jit(solution)/shard_map/ppermute | solution.py:26
  151.0 0.0 slice-start
  151.0 0.0 slice-start.1
  151.0 0.0 copy-start.1
  151.0 2.4 collective-permute-start.10
  153.4 1.5 copy-done.5
  154.9 4.5 %shard_map.70.weight = f32[768,768]{1,0:T(8,128)S(1)} custom-call(s32[4,32,2]{2,1,0:T(8,128)S(1)} %copy.15.offs, s32[4,1]{1,0:T(4,128)S(1)} %slice.30.refs_7_.cnt, f32[2,256,256]{2,1,0:T(8,128)S(1)} %copy-done.5), custom_call_target="tpu_custom_call" | custom-call | flops 8589934592 | bytes 20971520 | tf_op jit(solution)/shard_map/pallas_call | solution.py:242
  159.4 0.0 collective-permute-done.8.side_2
  159.4 0.0 collective-permute-done.7.side_1
  159.4 0.0 slice-done
  159.4 0.0 slice-done.1
  159.5 0.0 copy-done.1
  159.5 6.6 %shard_map.71.partial = f32[2,768,768]{2,1,0:T(8,128)} custom-call(f32[2,768,768]{2,1,0:T(8,128)S(1)} %bitcast.17, f32[2,768,1024]{2,1,0:T(8,128)} %get-tuple-element.9.acc_1, f32[2,512,1024]{2,1,0:T(8,128)S(1)} %copy-done.1, f32[2,768,256]{2,1,0:T(8,128)} %collective-permute-done.7.side_1, f32[2,256,256]{2,1,0:T(8,128)S(1)} %collective-permute-done.8.side_2, ...), custom_call_target="tpu_custom_call" | custom-call | flops 8388608 | bytes 23068672 | tf_op jit(solution)/shard_map/pallas_call | solution.py:279
  166.1 108.4 %all-reduce.2.cloned.1.call-done.totals = f32[3,256,256]{2,1,0:T(8,128)} async-done(((f32[3,256,256]{2,1,0:T(8,128)}), f32[3,256,256]{2,1,0:T(8,128)}) %all-reduce.2.cloned.1.call-update) | async-done | bytes 786448 | tf_op jit(solution)/shard_map/psum | solution.py:383
  274.4 0.0 collective-permute-done.11.lower_b
  274.4 0.0 collective-permute-done.10.lower_a
  274.5 2.3 copy-done
  276.8 1.1 copy-done.2
  277.9 3.1 %shard_map.72 = (f32[2,768,768]{2,1,0:T(8,128)}, f32[2,256,256]{2,1,0:T(8,128)}) custom-call(f32[2,768,768]{2,1,0:T(8,128)} %shard_map.71.partial, f32[2,768,768]{2,1,0:T(8,128)S(1)} %bitcast.18, f32[2,256,256]{2,1,0:T(8,128)} %collective-permute-done.10.lower_a, ...), custom_call_target="tpu_custom_call", output_to_operand_aliasing={{0}: (0, {})} | custom-call | flops 4194304 | bytes 10485760 | tf_op jit(solution)/shard_map/pallas_call | solution.py:315
  (5 shorter events, 0.0 us)
Async XLA Ops:
  7.2 267.3 %all-reduce.2.cloned.1.call-start = ((), (), s32[]{:S(2)}) async-start(), calls=%async_computation | async-start | bytes 1572864 | tf_op jit(solution)/shard_map/psum | solution.py:383
  7.2 24.4 %copy-start.4 = (f32[2,256,256]{2,1,0:T(8,128)S(1)}, f32[2,256,256]{2,1,0:T(8,128)}, u32[]{:S(2)}) copy-start(f32[2,256,256]{2,1,0:T(8,128)} %probe.1) | copy-start | bytes 1572868
  9.9 21.6 %collective-permute-start.3 = (f32[2,768,256]{2,1,0:T(8,128)}, f32[2,768,256]{2,1,0:T(8,128)S(1)}, u32[]{:S(2)}, u32[]{:S(2)}) collective-permute-start(f32[2,768,256]{2,1,0:T(8,128)} %slice.40), channel_id=1, source_target_pairs={{1,0},{2,1},{3,2},{4,3},{5,4},{6,5},{7,6},{9,8},{10,9},{11,10},{12... | collective-permute-start | bytes 4718600 | tf_op jit(solution)/shard_map/ppermute | solution.py:26
  12.1 19.5 %copy-start.3 = (bf16[32,256,256]{2,1,0:T(8,128)(2,1)S(1)}, bf16[32,256,256]{2,1,0:T(8,128)(2,1)}, u32[]{:S(2)}) copy-start(bf16[32,256,256]{2,1,0:T(8,128)(2,1)} %refs_5_.3) | copy-start | bytes 12582916
  13.0 17.1 %collective-permute-start = (s32[65]{0:T(128)S(1)}, s32[65]{0:T(128)S(1)}, u32[]{:S(2)}, u32[]{:S(2)}) collective-permute-start(s32[65]{0:T(128)S(1)} %pad_add_fusion.1), channel_id=1, source_target_pairs={{0,1},{1,2},{2,3},{3,4},{4,5},{5,6},{6,7},{8,9},{9,10},{10,11},{11... | collective-permute-start | bytes 788 | tf_op jit(solution)/shard_map/ppermute | solution.py:26
  16.1 15.3 %collective-permute-start.1 = (s32[65]{0:T(128)S(1)}, s32[65]{0:T(128)S(1)}, u32[]{:S(2)}, u32[]{:S(2)}) collective-permute-start(s32[65]{0:T(128)S(1)} %pad_add_fusion.1), channel_id=1, source_target_pairs={{0,8},{1,9},{2,10},{3,11},{4,12},{5,13},{6,14},{7,15},{16,24},{17,... | collective-permute-start | bytes 788 | tf_op jit(solution)/shard_map/ppermute | solution.py:26
  22.1 9.3 %collective-permute-start.2 = (s32[65]{0:T(128)S(1)}, s32[65]{0:T(128)S(1)}, u32[]{:S(2)}, u32[]{:S(2)}) collective-permute-start(s32[65]{0:T(128)S(1)} %pad_add_fusion.1), channel_id=1, source_target_pairs={{0,9},{1,10},{2,11},{3,12},{4,13},{5,14},{6,15},{16,25},{17,26},{1... | collective-permute-start | bytes 788 | tf_op jit(solution)/shard_map/ppermute | solution.py:26
  25.2 51.3 %collective-permute-start.4 = (f32[2,256,256]{2,1,0:T(8,128)S(1)}, f32[2,256,256]{2,1,0:T(8,128)S(1)}, u32[]{:S(2)}, u32[]{:S(2)}) collective-permute-start(f32[2,256,256]{2,1,0:T(8,128)S(1)} %slice.41), channel_id=1, source_target_pairs={{8,0},{9,1},{10,2},{11,3},{12,4},{13,5},{14,6},{15,7},{24,16},{25,... | collective-permute-start | bytes 1572872 | tf_op jit(solution)/shard_map/ppermute | solution.py:26
  30.1 68.4 %collective-permute-start.5 = (f32[2,256,512]{2,1,0:T(8,128)S(1)}, f32[2,256,512]{2,1,0:T(8,128)S(1)}, u32[]{:S(2)}, u32[]{:S(2)}) collective-permute-start(f32[2,256,512]{2,1,0:T(8,128)S(1)} %slice.42), channel_id=1, source_target_pairs={{8,0},{9,1},{10,2},{11,3},{12,4},{13,5},{14,6},{15,7},{24,16},{25,... | collective-permute-start | bytes 3145736 | tf_op jit(solution)/shard_map/ppermute | solution.py:26
  77.2 21.3 %collective-permute-start.6 = (f32[2,256,256]{2,1,0:T(8,128)S(1)}, f32[2,256,256]{2,1,0:T(8,128)S(1)}, u32[]{:S(2)}, u32[]{:S(2)}) collective-permute-start(f32[2,256,256]{2,1,0:T(8,128)S(1)} %broadcast_multiply_fusion), channel_id=1, source_target_pairs={{1,0},{2,1},{3,2},{4,3},{5,4},{6,5},{7,6},{9,8},{10,9},{11,10},{12... | collective-permute-start | bytes 1572872 | tf_op jit(solution)/shard_map/ppermute | solution.py:26
  115.9 24.1 %collective-permute-start.9 = (f32[2,256,256]{2,1,0:T(8,128)S(1)}, f32[2,256,256]{2,1,0:T(8,128)S(1)}, u32[]{:S(2)}, u32[]{:S(2)}) collective-permute-start(f32[2,256,256]{2,1,0:T(8,128)S(1)} %slice.38), channel_id=1, source_target_pairs={{0,1},{1,2},{2,3},{3,4},{4,5},{5,6},{6,7},{8,9},{9,10},{10,11},{11... | collective-permute-start | bytes 1572872 | tf_op jit(solution)/shard_map/ppermute | solution.py:26
  120.0 39.4 %collective-permute-start.7 = (f32[2,768,256]{2,1,0:T(8,128)}, f32[2,768,256]{2,1,0:T(8,128)}, u32[]{:S(2)}, u32[]{:S(2)}) collective-permute-start(f32[2,768,256]{2,1,0:T(8,128)} %slice.34), channel_id=1, source_target_pairs={{0,1},{1,2},{2,3},{3,4},{4,5},{5,6},{6,7},{8,9},{9,10},{10,11},{11... | collective-permute-start | bytes 4718600 | tf_op jit(solution)/shard_map/ppermute | solution.py:26
  132.1 142.3 %collective-permute-start.11 = (f32[2,256,512]{2,1,0:T(8,128)}, f32[2,256,512]{2,1,0:T(8,128)S(1)}, u32[]{:S(2)}, u32[]{:S(2)}) collective-permute-start(f32[2,256,512]{2,1,0:T(8,128)} %slice.39), channel_id=1, source_target_pairs={{0,8},{1,9},{2,10},{3,11},{4,12},{5,13},{6,14},{7,15},{16,24},{17,... | collective-permute-start | bytes 3145736 | tf_op jit(solution)/shard_map/ppermute | solution.py:26
  142.2 17.2 %collective-permute-start.8 = (f32[2,256,256]{2,1,0:T(8,128)S(1)}, f32[2,256,256]{2,1,0:T(8,128)S(1)}, u32[]{:S(2)}, u32[]{:S(2)}) collective-permute-start(f32[2,256,256]{2,1,0:T(8,128)S(1)} %get-tuple-element.17), channel_id=1, source_target_pairs={{0,1},{1,2},{2,3},{3,4},{4,5},{5,6},{6,7},{8,9},{9,10},{10,11},{11... | collective-permute-start | bytes 1572872 | tf_op jit(solution)/shard_map/ppermute | solution.py:26
  151.0 8.5 %slice-start = ((s8[4718592]{0:T(1024)(128)(4,1)}), s8[4194304]{0:T(1024)(128)(4,1)S(1)}, s32[]{:S(2)}) async-start(s8[4718592]{0:T(1024)(128)(4,1)} %bitcast.15), calls=%async_computation.1 | async-start | bytes 8388608
  151.0 8.5 %slice-start.1 = ((s8[4718592]{0:T(1024)(128)(4,1)}), s8[524288]{0:T(1024)(128)(4,1)S(1)}, s32[]{:S(2)}) async-start(s8[4718592]{0:T(1024)(128)(4,1)} %bitcast.15), calls=%async_computation.2 | async-start | bytes 1048576
  151.0 8.5 %copy-start.1 = (f32[2,512,1024]{2,1,0:T(8,128)S(1)}, f32[2,512,1024]{2,1,0:T(8,128)}, u32[]{:S(2)}) copy-start(f32[2,512,1024]{2,1,0:T(8,128)} %get-tuple-element.12.acc_2) | copy-start | bytes 12582916
  151.0 123.5 %collective-permute-start.10 = (f32[2,256,256]{2,1,0:T(8,128)}, f32[2,256,256]{2,1,0:T(8,128)}, u32[]{:S(2)}, u32[]{:S(2)}) collective-permute-start(f32[2,256,256]{2,1,0:T(8,128)} %get-tuple-element.16), channel_id=1, source_target_pairs={{0,8},{1,9},{2,10},{3,11},{4,12},{5,13},{6,14},{7,15},{16,24},{17,... | collective-permute-start | bytes 1572872 | tf_op jit(solution)/shard_map/ppermute | solution.py:26
  153.4 1.5 copy-start.5
  274.5 2.3 copy-start
  276.8 1.1 copy-start.2
Sparse Core Ops, SparseCore 0:
  140.2 134.2 all-reduce.1

commit v2 on v1

--- a/solution.py
+++ b/solution.py
@@ -24,6 +24,21 @@
         if 0 <= row < 2 and 0 <= col < cols:
             pairs.append((source, row * cols + col))
     return lax.ppermute(value, axis, pairs)
+
+
+def summed(value, axis):
+    count = lax.axis_size(axis)
+    odd = lax.axis_index(axis) % 2 == 1
+    rows = value.shape[1] // 2
+    swap = [(source, source + 1 - 2 * (source % 2)) for source in range(count)]
+    upper, lower = value[:, :rows], value[:, rows:]
+    got = lax.ppermute(jnp.where(odd, upper, lower), axis, swap)
+    half = jnp.where(odd, lower, upper) + got
+    groups = [list(range(0, count, 2)), list(range(1, count, 2))]
+    half = lax.psum(half, axis, axis_index_groups=groups)
+    other = lax.ppermute(half, axis, swap)
+    first, second = jnp.where(odd, other, half), jnp.where(odd, half, other)
+    return jnp.concatenate([first, second], axis=1)
 
 
 def dft_tables(window):
@@ -380,7 +395,7 @@
     )
     below = passed_along(acc_2[:, window:, tile:], "tile", 0, 1)
     lower_b = passed_along(acc_2[:, window:, window:tile], "tile", 1, 0)
-    totals = lax.psum(sums, "tile")
+    totals = summed(sums, "tile")
     lower_a = passed_along(acc_2[:, window:, :window] + below, "tile", 1, 0)
     side_2 = passed_along(acc_2[:, :window, tile:], "tile", 0, 1)
     partial = join(object_tile, acc_1, acc_2, side_1, side_2, weight)

time: 289 us -> 289 us (level)
  Pallas kernels: 56.4 us -> 92.8 us
  waiting for transfers between devices: 148 us -> 121 us
  starting transfers between devices: 46.1 us -> 26 us
  local copies, waits for them, and re-layouts: 17.7 us -> 24.4 us
    pallas_call x2, Pallas kernels: 42.1 us -> 76.1 us  [run_patterns(): pl.pallas_call(functools.partial(pattern_kernel, plan, window, row_base,...]
    ppermute x12, starting transfers between devices: 46 us -> 25.8 us  [passed_along(): return lax.ppermute(value, axis, pairs)]
    ppermute x12, waiting for transfers between devices: 39.1 us -> 19.6 us  [passed_along(): return lax.ppermute(value, axis, pairs)]
    psum x1, waiting for transfers between devices: 108 us -> 102 us  [summed(): half = lax.psum(half, axis, axis_index_groups=groups)]
    unnamed x17 -> x21, local copies, waits for them, and re-layouts: 5.74 us -> 10.7 us
  transfers between devices with their start and end apart: 13 -> 15, of which waited for: 3 -> 3; matrix products, arithmetic and copies ran while one was open for 5% -> 7% of each run, Pallas kernels for 13% -> 19%
where the time goes in v2:
time: 289 us; the launch traced here: 287 us
  waiting for transfers between devices  121 us (42%)
  Pallas kernels  92.8 us (32%)
  starting transfers between devices  26 us (9%)
  local copies, waits for them, and re-layouts  24.4 us (8%)
  between operations  15.2 us (5%)
  other arithmetic  7.16 us (2%)
    psum x1, waiting for transfers between devices, summed(): half = lax.psum(half, axis, axis_index_groups=groups)  102 us
    pallas_call x2, Pallas kernels, run_patterns(): pl.pallas_call(functools.partial(pattern_kernel, plan, window, row_base,...  76.1 us
    ppermute x12, starting transfers between devices, passed_along(): return lax.ppermute(value, axis, pairs)  25.8 us
    ppermute x12, waiting for transfers between devices, passed_along(): return lax.ppermute(value, axis, pairs)  19.6 us
    unnamed x21, local copies, waits for them, and re-layouts  10.7 us
    pallas_call x1, Pallas kernels, weights(): pl.pallas_call(functools.partial(weight_kernel, window, tile), out_shape=...  7.03 us
    pallas_call x1, Pallas kernels, join(): pl.pallas_call(join_kernel, grid=(tile // window,), out_shape=jax.ShapeDt...  6.54 us
  transfers between devices with their start and end apart: 15, of which 3 were waited for; matrix products, arithmetic and copies ran while one was open for 7% of the time, Pallas kernels for 19%

profile of v2, /device:TPU:0, one launch (start us, length us, event | category | flops | bytes accessed | tf_op | source)
XLA Modules:
  0.0 286.9 jit_solution(9465970273010663451)
XLA Ops:
  7.2 0.0 all-reduce.2.cloned.1.call-start
  7.2 2.7 slice.48
  9.9 1.3 collective-permute-start.3
  11.2 0.8 copy.12.refs_0_
  11.9 0.1 reshape.10
  12.0 0.0 copy-start.3
  12.8 0.1 pad_add_fusion.1
  12.9 3.1 %collective-permute-start = (s32[65]{0:T(128)S(1)}, s32[65]{0:T(128)S(1)}, u32[]{:S(2)}, u32[]{:S(2)}) collective-permute-start(s32[65]{0:T(128)S(1)} %pad_add_fusion.1), channel_id=1, source_target_pairs={{0,1},{1,2},{2,3},{3,4},{4,5},{5,6},{6,7},{8,9},{9,10},{10,11},{11... | collective-permute-start | bytes 788 | tf_op jit(solution)/shard_map/ppermute | solution.py:26
  16.1 5.9 %collective-permute-start.1 = (s32[65]{0:T(128)S(1)}, s32[65]{0:T(128)S(1)}, u32[]{:S(2)}, u32[]{:S(2)}) collective-permute-start(s32[65]{0:T(128)S(1)} %pad_add_fusion.1), channel_id=1, source_target_pairs={{0,8},{1,9},{2,10},{3,11},{4,12},{5,13},{6,14},{7,15},{16,24},{17,... | collective-permute-start | bytes 788 | tf_op jit(solution)/shard_map/ppermute | solution.py:26
  22.0 2.0 collective-permute-start.2
  24.1 1.1 slice.49
  25.1 1.3 collective-permute-start.4
  26.4 1.0 fusion.8
  27.4 1.1 multiply_convert_fusion
  28.6 0.1 fusion.1
  28.6 0.1 fusion.9
  28.7 2.3 slice.50
  31.0 0.0 collective-permute-done
  31.0 1.3 collective-permute-start.5
  32.3 0.0 collective-permute-done.1
  32.3 0.1 slice.36.refs_7_.cnt
  32.4 0.0 collective-permute-done.3.refs_9_
  32.4 0.1 broadcast_in_dim.8.refs_6_
  32.5 0.0 copy-start.4
  32.5 1.0 copy-done.4
  33.5 41.8 %shard_map.68 = (f32[2,768,1024]{2,1,0:T(8,128)}, f32[3,256,256]{2,1,0:T(8,128)S(1)}, f32[1,1]{1,0:T(1,128)}) custom-call(s32[32,2]{1,0:T(8,128)S(1)} %copy.12.refs_0_, s32[1]{0:T(128)S(6)} %copy.18.refs_1_, f32[2,256,256]{2,1,0:T(8,128)S(1)} %copy-done.4, bf16[512,512]{1,0:T(8,128)(2,1)S(1)} %get-tuple-element.21.refs_3_, ...), custom_call_target="tpu_custom_call" | custom-call | flops 8589934592 | bytes 31457280 | tf_op jit(solution)/shard_map/pallas_call | solution.py:187
  75.3 0.0 copy-start.7
  75.3 0.9 copy-done.7
  76.2 0.3 collective-permute-done.4.refs_10_
  76.4 1.5 broadcast_multiply_fusion
  77.9 1.3 collective-permute-start.6
  79.2 19.3 %collective-permute-done.5.refs_11_ = f32[2,256,512]{2,1,0:T(8,128)} collective-permute-done((f32[2,256,512]{2,1,0:T(8,128)}, f32[2,256,512]{2,1,0:T(8,128)}, u32[]{:S(2)}, u32[]{:S(2)}) %collective-permute-start.5) | collective-permute-done | bytes 1048608 | tf_op jit(solution)/shard_map/ppermute | solution.py:26
  98.5 1.0 copy-done.5
  99.5 1.1 copy-done.8
  100.7 34.3 %shard_map.69 = (f32[2,512,1024]{2,1,0:T(8,128)}, f32[3,256,256]{2,1,0:T(8,128)S(1)}, f32[1,1]{1,0:T(1,128)}) custom-call(s32[32,2]{1,0:T(8,128)S(1)} %copy.12.refs_0_, s32[1]{0:T(128)S(6)} %copy.18.refs_1_, f32[2,256,256]{2,1,0:T(8,128)S(1)} %copy-done.5, bf16[512,512]{1,0:T(8,128)(2,1)S(1)} %get-tuple-element.21.refs_3_, ...), custom_call_target="tpu_custom_call" | custom-call | flops 8589934592 | bytes 31457280 | tf_op jit(solution)/shard_map/pallas_call | solution.py:187
  135.0 0.1 slice_select_fusion
  135.1 0.1 collective-permute-start.12
  135.1 1.9 slice.44
  137.0 2.4 collective-permute-start.9
  139.4 2.7 slice.40
  142.1 2.0 collective-permute-start.7
  144.1 0.0 collective-permute-done.12
  144.1 0.8 select_add_fusion
  144.9 0.0 all-reduce.2.cloned.1.call-update
  144.9 0.1 copy.14
  145.0 0.3 copy.15.offs
  145.4 2.4 slice.45
  147.8 1.3 collective-permute-start.11
  149.2 2.3 slice_add_fusion
  151.5 2.5 collective-permute-start.8
  154.1 1.3 collective-permute-start.10
  155.4 101.9 %all-reduce.2.cloned.1.call-done = f32[3,128,256]{2,1,0:T(8,128)} async-done(((f32[3,128,256]{2,1,0:T(8,128)}), f32[3,128,256]{2,1,0:T(8,128)}) %all-reduce.2.cloned.1.call-update) | async-done | bytes 393232 | tf_op jit(solution)/shard_map/psum | solution.py:38
  257.3 1.2 copy-done.6
  258.5 7.0 %shard_map.70.weight = f32[768,768]{1,0:T(8,128)S(1)} custom-call(s32[4,32,2]{2,1,0:T(8,128)S(1)} %copy.15.offs, s32[4,1]{1,0:T(4,128)S(1)} %slice.36.refs_7_.cnt, f32[2,256,256]{2,1,0:T(8,128)S(1)} %copy-done.6), custom_call_target="tpu_custom_call" | custom-call | flops 8589934592 | bytes 20971520 | tf_op jit(solution)/shard_map/pallas_call | solution.py:257
  265.5 0.0 collective-permute-done.8.side_2
  265.5 0.0 copy-start
  265.5 2.3 copy-done
  267.9 6.5 %shard_map.71.partial = f32[2,768,768]{2,1,0:T(8,128)} custom-call(f32[2,768,768]{2,1,0:T(8,128)S(1)} %bitcast.15, f32[2,768,1024]{2,1,0:T(8,128)} %get-tuple-element.9.acc_1, f32[2,512,1024]{2,1,0:T(8,128)S(1)} %copy-done.2, f32[2,768,256]{2,1,0:T(8,128)S(1)} %collective-permute-done.7.side_1, f32[2,256,256]{2,1,0:T(8,128)} %collective-permute-done.8.side_2, ...), custom_call_target="tpu_custom_call" | custom-call | flops 8388608 | bytes 23068672 | tf_op jit(solution)/shard_map/pallas_call | solution.py:294
  274.4 0.1 broadcast_select_fusion.1
  274.5 0.1 pad_maximum_fusion.totals
  274.6 0.0 collective-permute-done.10.lower_a
  274.6 0.0 copy-start.1
  274.6 2.3 copy-done.1
  276.9 3.1 %shard_map.72 = (f32[2,768,768]{2,1,0:T(8,128)}, f32[2,256,256]{2,1,0:T(8,128)}) custom-call(f32[2,768,768]{2,1,0:T(8,128)} %shard_map.71.partial, f32[2,768,768]{2,1,0:T(8,128)S(1)} %bitcast.16, f32[2,256,256]{2,1,0:T(8,128)S(1)} %collective-permute-done.10.lower_a, ...), custom_call_target="tpu_custom_call", output_to_operand_aliasing={{0}: (0, {})} | custom-call | flops 4194304 | bytes 10485760 | tf_op jit(solution)/shard_map/pallas_call | solution.py:330
  (16 shorter events, 0.0 us)
Async XLA Ops:
  7.2 250.1 %all-reduce.2.cloned.1.call-start = ((), (), s32[]{:S(2)}) async-start(), calls=%async_computation | async-start | bytes 786432 | tf_op jit(solution)/shard_map/psum | solution.py:38
  9.9 22.5 %collective-permute-start.3 = (f32[2,768,256]{2,1,0:T(8,128)}, f32[2,768,256]{2,1,0:T(8,128)S(1)}, u32[]{:S(2)}, u32[]{:S(2)}) collective-permute-start(f32[2,768,256]{2,1,0:T(8,128)} %slice.48), channel_id=1, source_target_pairs={{1,0},{2,1},{3,2},{4,3},{5,4},{6,5},{7,6},{9,8},{10,9},{11,10},{12... | collective-permute-start | bytes 4718600 | tf_op jit(solution)/shard_map/ppermute | solution.py:26
  12.0 20.4 %copy-start.3 = (bf16[32,256,256]{2,1,0:T(8,128)(2,1)S(1)}, bf16[32,256,256]{2,1,0:T(8,128)(2,1)}, u32[]{:S(2)}) copy-start(bf16[32,256,256]{2,1,0:T(8,128)(2,1)} %refs_5_.3) | copy-start | bytes 12582916
  12.9 18.1 %collective-permute-start = (s32[65]{0:T(128)S(1)}, s32[65]{0:T(128)S(1)}, u32[]{:S(2)}, u32[]{:S(2)}) collective-permute-start(s32[65]{0:T(128)S(1)} %pad_add_fusion.1), channel_id=1, source_target_pairs={{0,1},{1,2},{2,3},{3,4},{4,5},{5,6},{6,7},{8,9},{9,10},{10,11},{11... | collective-permute-start | bytes 788 | tf_op jit(solution)/shard_map/ppermute | solution.py:26
  16.1 16.2 %collective-permute-start.1 = (s32[65]{0:T(128)S(1)}, s32[65]{0:T(128)S(1)}, u32[]{:S(2)}, u32[]{:S(2)}) collective-permute-start(s32[65]{0:T(128)S(1)} %pad_add_fusion.1), channel_id=1, source_target_pairs={{0,8},{1,9},{2,10},{3,11},{4,12},{5,13},{6,14},{7,15},{16,24},{17,... | collective-permute-start | bytes 788 | tf_op jit(solution)/shard_map/ppermute | solution.py:26
  22.0 10.3 %collective-permute-start.2 = (s32[65]{0:T(128)S(1)}, s32[65]{0:T(128)S(1)}, u32[]{:S(2)}, u32[]{:S(2)}) collective-permute-start(s32[65]{0:T(128)S(1)} %pad_add_fusion.1), channel_id=1, source_target_pairs={{0,9},{1,10},{2,11},{3,12},{4,13},{5,14},{6,15},{16,25},{17,26},{1... | collective-permute-start | bytes 788 | tf_op jit(solution)/shard_map/ppermute | solution.py:26
  25.1 51.3 %collective-permute-start.4 = (f32[2,256,256]{2,1,0:T(8,128)S(1)}, f32[2,256,256]{2,1,0:T(8,128)S(1)}, u32[]{:S(2)}, u32[]{:S(2)}) collective-permute-start(f32[2,256,256]{2,1,0:T(8,128)S(1)} %slice.49), channel_id=1, source_target_pairs={{8,0},{9,1},{10,2},{11,3},{12,4},{13,5},{14,6},{15,7},{24,16},{25,... | collective-permute-start | bytes 1572872 | tf_op jit(solution)/shard_map/ppermute | solution.py:26
  31.0 67.5 %collective-permute-start.5 = (f32[2,256,512]{2,1,0:T(8,128)}, f32[2,256,512]{2,1,0:T(8,128)}, u32[]{:S(2)}, u32[]{:S(2)}) collective-permute-start(f32[2,256,512]{2,1,0:T(8,128)} %slice.50), channel_id=1, source_target_pairs={{8,0},{9,1},{10,2},{11,3},{12,4},{13,5},{14,6},{15,7},{24,16},{25,... | collective-permute-start | bytes 3145736 | tf_op jit(solution)/shard_map/ppermute | solution.py:26
  32.5 1.0 copy-start.4
  75.3 0.9 copy-start.7
  77.9 20.6 %collective-permute-start.6 = (f32[2,256,256]{2,1,0:T(8,128)}, f32[2,256,256]{2,1,0:T(8,128)}, u32[]{:S(2)}, u32[]{:S(2)}) collective-permute-start(f32[2,256,256]{2,1,0:T(8,128)} %broadcast_multiply_fusion), channel_id=1, source_target_pairs={{1,0},{2,1},{3,2},{4,3},{5,4},{6,5},{7,6},{9,8},{10,9},{11,10},{12... | collective-permute-start | bytes 1572872 | tf_op jit(solution)/shard_map/ppermute | solution.py:26
  98.5 1.0 copy-start.5
  99.5 1.1 copy-start.8
  135.1 9.0 %collective-permute-start.12 = (f32[3,128,256]{2,1,0:T(8,128)S(1)}, f32[3,128,256]{2,1,0:T(8,128)S(1)}, u32[]{:S(2)}, u32[]{:S(2)}) collective-permute-start(f32[3,128,256]{2,1,0:T(8,128)S(1)} %slice_select_fusion), channel_id=1, source_target_pairs={{0,1},{1,0},{2,3},{3,2},{4,5},{5,4},{6,7},{7,6},{8,9},{9,8},{10,11... | collective-permute-start | bytes 1179656 | tf_op jit(solution)/shard_map/ppermute | solution.py:35
  137.0 12.2 %collective-permute-start.9 = (f32[2,256,256]{2,1,0:T(8,128)}, f32[2,256,256]{2,1,0:T(8,128)S(1)}, u32[]{:S(2)}, u32[]{:S(2)}) collective-permute-start(f32[2,256,256]{2,1,0:T(8,128)} %slice.44), channel_id=1, source_target_pairs={{0,1},{1,2},{2,3},{3,4},{4,5},{5,6},{6,7},{8,9},{9,10},{10,11},{11... | collective-permute-start | bytes 1572872 | tf_op jit(solution)/shard_map/ppermute | solution.py:26
  142.1 123.4 %collective-permute-start.7 = (f32[2,768,256]{2,1,0:T(8,128)}, f32[2,768,256]{2,1,0:T(8,128)S(1)}, u32[]{:S(2)}, u32[]{:S(2)}) collective-permute-start(f32[2,768,256]{2,1,0:T(8,128)} %slice.40), channel_id=1, source_target_pairs={{0,1},{1,2},{2,3},{3,4},{4,5},{5,6},{6,7},{8,9},{9,10},{10,11},{11... | collective-permute-start | bytes 4718600 | tf_op jit(solution)/shard_map/ppermute | solution.py:26
  147.8 126.8 %collective-permute-start.11 = (f32[2,256,512]{2,1,0:T(8,128)}, f32[2,256,512]{2,1,0:T(8,128)S(1)}, u32[]{:S(2)}, u32[]{:S(2)}) collective-permute-start(f32[2,256,512]{2,1,0:T(8,128)} %slice.45), channel_id=1, source_target_pairs={{0,8},{1,9},{2,10},{3,11},{4,12},{5,13},{6,14},{7,15},{16,24},{17,... | collective-permute-start | bytes 3145736 | tf_op jit(solution)/shard_map/ppermute | solution.py:26
  151.5 114.0 %collective-permute-start.8 = (f32[2,256,256]{2,1,0:T(8,128)}, f32[2,256,256]{2,1,0:T(8,128)}, u32[]{:S(2)}, u32[]{:S(2)}) collective-permute-start(f32[2,256,256]{2,1,0:T(8,128)} %get-tuple-element.17), channel_id=1, source_target_pairs={{0,1},{1,2},{2,3},{3,4},{4,5},{5,6},{6,7},{8,9},{9,10},{10,11},{11... | collective-permute-start | bytes 1572872 | tf_op jit(solution)/shard_map/ppermute | solution.py:26
  154.1 120.5 %collective-permute-start.10 = (f32[2,256,256]{2,1,0:T(8,128)}, f32[2,256,256]{2,1,0:T(8,128)S(1)}, u32[]{:S(2)}, u32[]{:S(2)}) collective-permute-start(f32[2,256,256]{2,1,0:T(8,128)} %get-tuple-element.16), channel_id=1, source_target_pairs={{0,8},{1,9},{2,10},{3,11},{4,12},{5,13},{6,14},{7,15},{16,24},{17,... | collective-permute-start | bytes 1572872 | tf_op jit(solution)/shard_map/ppermute | solution.py:26
  257.3 8.3 %copy-start.2 = (f32[2,512,1024]{2,1,0:T(8,128)S(1)}, f32[2,512,1024]{2,1,0:T(8,128)}, u32[]{:S(2)}) copy-start(f32[2,512,1024]{2,1,0:T(8,128)} %get-tuple-element.12.acc_2) | copy-start | bytes 12582916
  257.3 17.1 %collective-permute-start.13 = (f32[3,128,256]{2,1,0:T(8,128)}, f32[3,128,256]{2,1,0:T(8,128)S(1)}, u32[]{:S(2)}, u32[]{:S(2)}) collective-permute-start(f32[3,128,256]{2,1,0:T(8,128)} %all-reduce.2.cloned.1.call-done), channel_id=1, source_target_pairs={{0,1},{1,0},{2,3},{3,2},{4,5},{5,4},{6,7},{7,6},{8,9},{9,8},{10,11... | collective-permute-start | bytes 1179656 | tf_op jit(solution)/shard_map/ppermute | solution.py:39
  257.3 1.2 copy-start.6
  258.5 16.0 %copy-start.9 = (f32[3,128,256]{2,1,0:T(8,128)S(1)}, f32[3,128,256]{2,1,0:T(8,128)}, u32[]{:S(2)}) copy-start(f32[3,128,256]{2,1,0:T(8,128)} %all-reduce.2.cloned.1.call-done) | copy-start | bytes 1179652
  265.5 2.3 copy-start
  274.6 2.3 copy-start.1
Sparse Core Ops, SparseCore 0:
  145.1 112.1 all-reduce.1
